TPU v7x, 512 devices: a whole 4x8x8 slice. The times are simulated.
512 devices in a mesh: tm: 16 (over y, core), space: 32 (over x, z).
Axes of the slice: x: 4, y: 8, z: 8, core: 2. Of those that a mesh axis runs over, the one named last changes fastest.
Arguments:
- coupling: bfloat16 [16, 2048, 2048], P('tm', 'space'), may hold values from -0.125 to 0.125
- arrow_link: float32 [16, 2048, 64], P('tm'), may hold values from -0.75 to 0.75
- local_cov: float32 [16, 2048, 2048], P('tm', 'space'), as said below
- boundary_cov: float32 [16, 2048, 2048], P('tm', 'space'), as said below
- boundary_arrow: float32 [16, 2048, 64], P('tm', 'space'), may hold values from -6 to 6
- fixed_cov: float32 [64, 64], replicated, as said below
Outputs:
- diag_blocks: float32 [16, 2048, 2048], P('tm', 'space')
- cross_blocks: float32 [16, 2048, 2048], P('tm', 'space')
- arrow_covs: float32 [16, 2048, 64], P('tm', 'space')
Inputs may be any that keep to these rules, and one draw needn't show every extreme that they name: `local_cov`: each block is symmetric. `boundary_cov`: each block is symmetric. `fixed_cov`: symmetric.
All inputs are finite; a program needn't handle non-finite values.
Results may differ from a plain program's by a relative error of at most 0.0003.
Values may be sent and summed in bfloat16 or wider, within the bound.
No kernel may reach another device: no remote copies, remote signals or barrier semaphores. Data moves between devices by JAX's collectives and lax.ppermute only.
A program may use at most 64 MiB of HBM per device.

v0:
```python
import jax
import jax.numpy as jnp
from jax import lax
from jax.sharding import PartitionSpec as P


def passed_along(block, axis, distance):
    devices = range(lax.axis_size(axis))
    route = [(i - distance, i) for i in devices if i - distance in devices]
    return lax.ppermute(block, axis, route)


def shards(coupling, arrow_link, local_cov, boundary_cov, boundary_arrow, fixed_cov):
    highest = lax.Precision.HIGHEST
    next_block, next_arrow = passed_along((boundary_cov, boundary_arrow), "tm", -1)
    panels = lax.all_gather(coupling, "space", axis=1, tiled=True)[0]
    groups = lax.axis_size("space")
    rows_here = coupling.shape[1]
    offset = lax.axis_index("space") * rows_here
    link_block = arrow_link[0]
    link_rows = lax.dynamic_slice_in_dim(link_block, offset, rows_here, 0)
    succ_rows = next_block[0]
    succ_arrow = next_arrow[0]
    gathered = lax.all_gather(succ_arrow, "space", axis=0, tiled=True)
    carried = jnp.dot(coupling[0], gathered, precision=highest, preferred_element_type=jnp.float32)
    arrow_rows = carried + jnp.dot(
        link_rows, fixed_cov, precision=highest, preferred_element_type=jnp.float32
    )
    cross_turned = jnp.dot(
        succ_rows, panels.T, precision=highest, preferred_element_type=jnp.float32
    )
    cross_turned = cross_turned + jnp.dot(
        succ_arrow, link_block.T, precision=highest, preferred_element_type=jnp.float32
    )
    pieces = (
        cross_turned.reshape(rows_here, groups, rows_here)
        .transpose(2, 1, 0)
        .reshape(rows_here, groups * rows_here)
    )
    cross_rows = lax.all_to_all(pieces, "space", split_axis=1, concat_axis=1, tiled=True)
    diag_rows = local_cov[0] + jnp.dot(
        cross_rows, panels.T, precision=highest, preferred_element_type=jnp.float32
    )
    diag_rows = diag_rows + jnp.dot(
        arrow_rows, link_block.T, precision=highest, preferred_element_type=jnp.float32
    )
    return (diag_rows[None], cross_rows[None], arrow_rows[None])


def solution(mesh):
    return jax.shard_map(
        shards,
        mesh=mesh,
        in_specs=(
            P("tm", "space", None),
            P("tm", None, None),
            P("tm", "space", None),
            P("tm", "space", None),
            P("tm", "space", None),
            P(),
        ),
        out_specs=(P("tm", "space", None), P("tm", "space", None), P("tm", "space", None)),
        check_vma=False,
    )
```

profile of v0, /device:TPU:8, one launch (start us, length us, event | category | flops | bytes accessed | tf_op | source)
XLA Modules:
  0.0 218.1 jit_solution(1109246769169374447)
XLA Ops:
  7.2 0.0 copy-start
  7.2 0.0 copy-start.1
  7.2 0.0 copy-start.4
  7.2 0.0 all-gather.3.cloned.1.call-start
  7.2 0.7 all-gather.3.cloned.1.call-update
  7.9 1.9 collective-permute-start
  9.9 7.8 %collective-permute-start.1 = (f32[1,64,64]{2,1,0:T(8,128)}, f32[1,64,64]{2,1,0:T(8,128)S(1)}, u32[]{:S(2)}, u32[]{:S(2)}) collective-permute-start(f32[1,64,64]{2,1,0:T(8,128)} %param.10), channel_id=1, source_target_pairs={{32,0},{64,32},{96,64},{128,96},{160,128},{192,160},{224,192},{256... | collective-permute-start | bytes 49160 | tf_op jit(solution)/shard_map/ppermute | solution.py:10
  17.7 1.9 collective-permute-done.1
  19.6 0.0 copy-done
  19.6 0.6 fusion.13
  20.2 0.0 collective-permute-done
  20.2 100.1 %all-gather.3.cloned.1.call-done = bf16[1,2048,2048]{2,1,0:T(8,128)(2,1)} async-done(((bf16[1,64,2048]{2,1,0:T(8,128)(2,1)}), bf16[1,2048,2048]{2,1,0:T(8,128)(2,1)}) %all-gather.3.cloned.1.call-update) | async-done | bytes 8388624 | tf_op jit(solution)/shard_map/all_gather | solution.py:16
  120.3 10.0 %fusion.5 = f32[64,2048]{1,0:T(8,128)S(1)} fusion(f32[64,2048]{1,0:T(8,128)S(1)} %fusion.13, bf16[1,2048,2048]{2,1,0:T(8,128)(2,1)} %all-gather.3.cloned.1.call-done, f32[1,64,2048]{2,1,0:T(8,128)S(1)} %collective-permute-done), kind=kOutput, calls=%fused_computation.6 | convolution fusion | flops 3221356544 | bytes 9961472 | tf_op jit(solution)/shard_map/dot_general | solution.py:29
  130.4 0.0 copy-start.2
  130.4 0.3 copy.16
  130.7 1.5 reshape.17
  132.2 5.4 %all-to-all-start = ((f32[32,1,4096]{2,1,0:T(1,128)}), f32[32,1,4096]{2,1,0:T(1,128)S(1)}, u32[]{:S(2)}, u32[]{:S(2)}) async-start(f32[32,1,4096]{2,1,0:T(1,128)} %reshape.17), calls=%async_computation | async-start | bytes 1048576 | tf_op jit(solution)/shard_map/all_to_all | solution.py:40
  137.6 0.0 copy-done.4
  137.6 0.3 fusion.17
  138.0 56.4 %all-gather = f32[1,2048,64]{2,1,0:T(8,128)S(1)} all-gather(f32[1,64,64]{2,1,0:T(8,128)S(1)} %collective-permute-done.1), channel_id=2, replica_groups=mesh['tm'=16,'space'=32] {'space'}, dimensions={1}, use_global_device_ids=true | all-gather | bytes 540672 | tf_op jit(solution)/shard_map/all_gather | solution.py:24
  194.3 0.5 convolution_add_fusion.1
  194.8 0.0 copy-start.3
  194.8 0.0 all-to-all-done
  194.8 0.5 broadcast
  195.3 1.9 reduce
  197.2 0.4 reshape.18
  197.7 0.6 copy.14
  198.3 0.4 all_to_all.7
  198.6 1.2 broadcast_in_dim.10
  199.8 0.0 copy-done.2
  199.8 10.0 %fusion.8 = f32[64,2048]{1,0:T(8,128)S(1)} fusion(f32[64,2048]{1,0:T(8,128)S(1)} %all_to_all.7, bf16[1,2048,2048]{2,1,0:T(8,128)(2,1)} %all-gather.3.cloned.1.call-done, f32[1,64,2048]{2,1,0:T(8,128)S(1)} %copy-done.2), kind=kOutput, calls=%fused_computation.7 | convolution fusion | flops 3221356544 | bytes 9961472 | tf_op jit(solution)/shard_map/dot_general | solution.py:41
  209.9 1.4 fusion.4
  (2 shorter events, 0.0 us)
Async XLA Ops:
  7.2 12.4 %copy-start = (f32[1,2048,64]{1,2,0:T(8,128)S(1)}, f32[1,2048,64]{1,2,0:T(8,128)}, u32[]{:S(2)}) copy-start(f32[1,2048,64]{1,2,0:T(8,128)} %param.7) | copy-start | bytes 1572868
  7.2 187.1 %copy-start.1 = (bf16[1,64,2048]{2,1,0:T(8,128)(2,1)S(1)}, bf16[1,64,2048]{2,1,0:T(8,128)(2,1)}, u32[]{:S(2)}) copy-start(bf16[1,64,2048]{2,1,0:T(8,128)(2,1)} %param.6) | copy-start | bytes 786436
  7.2 130.4 %copy-start.4 = (f32[64,64]{1,0:T(8,128)S(1)}, f32[64,64]{1,0:T(8,128)}, u32[]{:S(2)}) copy-start(f32[64,64]{1,0:T(8,128)} %param.11) | copy-start | bytes 49156
  7.2 113.1 %all-gather.3.cloned.1.call-start = ((), (), s32[]{:S(2)}) async-start(), calls=%async_computation.1 | async-start | bytes 8650752 | tf_op jit(solution)/shard_map/all_gather | solution.py:16
  7.9 12.2 %collective-permute-start = (f32[1,64,2048]{2,1,0:T(8,128)}, f32[1,64,2048]{2,1,0:T(8,128)S(1)}, u32[]{:S(2)}, u32[]{:S(2)}) collective-permute-start(f32[1,64,2048]{2,1,0:T(8,128)} %param.9), channel_id=1, source_target_pairs={{32,0},{64,32},{96,64},{128,96},{160,128},{192,160},{224,192},{256... | collective-permute-start | bytes 1572872 | tf_op jit(solution)/shard_map/ppermute | solution.py:10
  9.9 9.7 %collective-permute-start.1 = (f32[1,64,64]{2,1,0:T(8,128)}, f32[1,64,64]{2,1,0:T(8,128)S(1)}, u32[]{:S(2)}, u32[]{:S(2)}) collective-permute-start(f32[1,64,64]{2,1,0:T(8,128)} %param.10), channel_id=1, source_target_pairs={{32,0},{64,32},{96,64},{128,96},{160,128},{192,160},{224,192},{256... | collective-permute-start | bytes 49160 | tf_op jit(solution)/shard_map/ppermute | solution.py:10
  130.4 69.4 %copy-start.2 = (f32[1,64,2048]{2,1,0:T(8,128)S(1)}, f32[1,64,2048]{2,1,0:T(8,128)}, u32[]{:S(2)}) copy-start(f32[1,64,2048]{2,1,0:T(8,128)} %param.8) | copy-start | bytes 1572868
  132.2 62.7 %all-to-all-start = ((f32[32,1,4096]{2,1,0:T(1,128)}), f32[32,1,4096]{2,1,0:T(1,128)S(1)}, u32[]{:S(2)}, u32[]{:S(2)}) async-start(f32[32,1,4096]{2,1,0:T(1,128)} %reshape.17), calls=%async_computation | async-start | bytes 1048576 | tf_op jit(solution)/shard_map/all_to_all | solution.py:40
  194.8 15.0 %copy-start.3 = (f32[64,64]{1,0:T(8,128)}, f32[64,64]{1,0:T(8,128)S(1)}, u32[]{:S(2)}) copy-start(f32[64,64]{1,0:T(8,128)S(1)} %convolution_add_fusion.1) | copy-start | bytes 49156
Sparse Core Ops, SparseCore 0:
  11.2 109.0 all-gather.2
where the time goes:
time: 218 us
  waiting for transfers between devices  103 us (47%)
  blocking collectives  56.4 us (26%)
  matrix products  22.8 us (10%)
  starting transfers between devices  15.2 us (7%)
  between operations  14.2 us (7%)
  local copies, waits for them, and re-layouts  4.86 us (2%)
    all_gather x1, waiting for transfers between devices, shards(): panels = lax.all_gather(coupling, 'space', axis=1, tiled=True)[0]  100 us
    all_gather x1, blocking collectives, shards(): gathered = lax.all_gather(succ_arrow, 'space', axis=0, tiled=True)  56.4 us
    dot_general x1, matrix products, shards(): jnp.dot(cross_rows, panels.T, precision=highest, preferred_element_type=j...  10 us
    dot_general x1, matrix products, shards(): jnp.dot(succ_rows, panels.T, precision=highest, preferred_element_type=jn...  10 us
    ppermute x2, starting transfers between devices, passed_along(): return lax.ppermute(block, axis, route)  9.75 us
    all_to_all x1, starting transfers between devices, shards(): lax.all_to_all(pieces, 'space', split_axis=1, concat_axis=1, tiled=True)  5.45 us
  transfers between devices with their start and end apart: 4, of which 2 were waited for; matrix products, arithmetic and copies ran while one was open for 1% of the time, Pallas kernels for 0%

commit v1 on v0

--- a/solution.py
+++ b/solution.py
@@ -2,6 +2,11 @@
 import jax.numpy as jnp
 from jax import lax
 from jax.sharding import PartitionSpec as P
+
+
+def gather_from_all(x, axis, dim):
+    copies = jnp.concatenate([x] * lax.axis_size(axis), axis=dim)
+    return lax.all_to_all(copies, axis, dim, dim, tiled=True)
 
 
 def passed_along(block, axis, distance):
@@ -13,7 +18,7 @@
 def shards(coupling, arrow_link, local_cov, boundary_cov, boundary_arrow, fixed_cov):
     highest = lax.Precision.HIGHEST
     next_block, next_arrow = passed_along((boundary_cov, boundary_arrow), "tm", -1)
-    panels = lax.all_gather(coupling, "space", axis=1, tiled=True)[0]
+    panels = gather_from_all(coupling, "space", 1)[0]
     groups = lax.axis_size("space")
     rows_here = coupling.shape[1]
     offset = lax.axis_index("space") * rows_here

time: 218 us -> 480 us (2.20)
  the two profiles are of different devices: /device:TPU:8 before, /device:TPU:32 now
where the time goes in v1:
time: 480 us; the launch traced here: 478 us
  waiting for transfers between devices  184 us (38%)
  local copies, waits for them, and re-layouts  115 us (24%)
  blocking collectives  55.9 us (12%)
  other arithmetic  52.9 us (11%)
  matrix products  37.8 us (8%)
  starting transfers between devices  32 us (7%)
    all_to_all x1, waiting for transfers between devices, gather_from_all(): return lax.all_to_all(copies, axis, dim, dim, tiled=True)  179 us
    unnamed x50, local copies, waits for them, and re-layouts  63.3 us
    all_gather x1, blocking collectives, shards(): gathered = lax.all_gather(succ_arrow, 'space', axis=0, tiled=True)  55.9 us
    unnamed x1, other arithmetic  51 us
    concatenate x2, local copies, waits for them, and re-layouts, gather_from_all(): copies = jnp.concatenate([x] * lax.axis_size(axis), axis=dim)  48.4 us
    dot_general x1, matrix products, shards(): jnp.dot(cross_rows, panels.T, precision=highest, preferred_element_type=j...  17.6 us
    dot_general x1, matrix products, shards(): jnp.dot(succ_rows, panels.T, precision=highest, preferred_element_type=jn...  17.5 us
    all_to_all x1, starting transfers between devices, shards(): lax.all_to_all(pieces, 'space', split_axis=1, concat_axis=1, tiled=True)  14 us
  transfers between devices with their start and end apart: 4, of which 2 were waited for; matrix products, arithmetic and copies ran while one was open for 5% of the time, Pallas kernels for 0%

profile of v1, /device:TPU:32, one launch (start us, length us, event | category | flops | bytes accessed | tf_op | source)
XLA Modules:
  0.0 477.9 jit_solution(16665585379537528735)
XLA Ops:
  0.7 1.0 constant_dynamic-update-slice_fusion.31
  1.7 1.0 constant_dynamic-update-slice_fusion.30
  2.7 1.0 constant_dynamic-update-slice_fusion.29
  3.6 1.0 constant_dynamic-update-slice_fusion.28
  4.6 1.0 constant_dynamic-update-slice_fusion.27
  5.6 1.0 constant_dynamic-update-slice_fusion.26
  6.6 1.0 constant_dynamic-update-slice_fusion.25
  7.5 1.0 constant_dynamic-update-slice_fusion.24
  8.5 1.0 constant_dynamic-update-slice_fusion.23
  9.5 1.0 constant_dynamic-update-slice_fusion.22
  10.5 1.0 constant_dynamic-update-slice_fusion.21
  11.4 1.0 constant_dynamic-update-slice_fusion.20
  12.4 1.0 constant_dynamic-update-slice_fusion.19
  13.4 1.0 constant_dynamic-update-slice_fusion.18
  14.3 1.0 constant_dynamic-update-slice_fusion.17
  16.7 48.3 %copy.101 = bf16[1,2048,2048]{2,0,1:T(2,128)(2,1)} copy(bf16[1,2048,2048]{2,1,0:T(8,128)(2,1)S(1)} %constant_dynamic-update-slice_fusion) | data formatting | bytes 16777216 | tf_op jit(solution)/shard_map/concatenate | solution.py:8
  65.6 51.0 %reduce = bf16[2048,2048]{1,0:T(8,128)(2,1)} reduce(bf16[2048,1,2048]{2,1,0:T(2,128)(2,1)} %bitcast.54, bf16[]{:T(256)} %broadcast), dimensions={1}, to_apply=%bitcast.51.reduce_sub_computation | reduce | bytes 16777218
  116.6 21.6 %reshape.17 = bf16[32,2,65536]{2,1,0:T(2,128)(2,1)} reshape(bf16[2048,2048]{1,0:T(8,128)(2,1)} %reduce) | data formatting | bytes 16777216
  138.2 13.4 %all-to-all-start = ((bf16[32,2,65536]{2,1,0:T(2,128)(2,1)}), bf16[32,2,65536]{2,1,0:T(2,128)(2,1)}, u32[]{:S(2)}, u32[]{:S(2)}) async-start(bf16[32,2,65536]{2,1,0:T(2,128)(2,1)} %reshape.17), calls=%async_computation | async-start | bytes 16777216 | tf_op jit(solution)/shard_map/all_to_all | solution.py:9
  151.7 1.9 collective-permute-start
  153.6 2.6 collective-permute-start.1
  156.3 4.4 collective-permute-done.1
  161.2 179.3 %all-to-all-done = bf16[32,2,65536]{2,1,0:T(2,128)(2,1)} async-done(((bf16[32,2,65536]{2,1,0:T(2,128)(2,1)}), bf16[32,2,65536]{2,1,0:T(2,128)(2,1)}, u32[]{:S(2)}, u32[]{:S(2)}) %all-to-all-start) | async-done | bytes 8388640 | tf_op jit(solution)/shard_map/all_to_all | solution.py:9
  340.5 23.4 %reshape.18 = bf16[2048,1,2048]{2,1,0:T(2,128)(2,1)} reshape(bf16[32,2,65536]{2,1,0:T(2,128)(2,1)} %all-to-all-done) | data formatting | bytes 16777216
  363.9 17.5 %fusion.10 = f32[64,2048]{1,0:T(8,128)S(1)} fusion(f32[64,2048]{1,0:T(8,128)S(1)} %fusion.18, bf16[1,2048,2048]{2,0,1:T(2,128)(2,1)} %bitcast.52, f32[1,64,2048]{2,1,0:T(8,128)S(1)} %collective-permute-done), kind=kOutput, calls=%fused_computation.9 | convolution fusion | flops 3221356544 | bytes 9961472 | tf_op jit(solution)/shard_map/dot_general | solution.py:34
  381.8 1.5 reshape.19
  383.2 14.0 %all-to-all-start.1 = ((f32[32,1,4096]{2,1,0:T(1,128)}), f32[32,1,4096]{2,1,0:T(1,128)S(1)}, u32[]{:S(2)}, u32[]{:S(2)}) async-start(f32[32,1,4096]{2,1,0:T(1,128)} %reshape.19), calls=%async_computation.1 | async-start | bytes 1048576 | tf_op jit(solution)/shard_map/all_to_all | solution.py:45
  397.5 55.9 %all-gather = f32[1,2048,64]{2,1,0:T(8,128)S(1)} all-gather(f32[1,64,64]{2,1,0:T(8,128)S(1)} %collective-permute-done.1), channel_id=2, replica_groups=mesh['tm'=16,'space'=32] {'space'}, dimensions={1}, use_global_device_ids=true | all-gather | bytes 540672 | tf_op jit(solution)/shard_map/all_gather | solution.py:29
  454.5 1.9 reduce.1
  457.8 1.2 broadcast_in_dim.10
  459.0 17.6 %fusion.13 = f32[64,2048]{1,0:T(8,128)S(1)} fusion(f32[64,2048]{1,0:T(8,128)S(1)} %all_to_all.11, bf16[1,2048,2048]{2,0,1:T(2,128)(2,1)} %bitcast.53, f32[1,64,2048]{2,1,0:T(8,128)S(1)} %copy-done.2), kind=kOutput, calls=%fused_computation.10 | convolution fusion | flops 3221356544 | bytes 9961472 | tf_op jit(solution)/shard_map/dot_general | solution.py:46
  476.5 1.4 fusion.9
  (42 shorter events, 5.4 us)
Async XLA Ops:
  0.6 160.0 %copy-start = (f32[1,2048,64]{1,2,0:T(8,128)S(1)}, f32[1,2048,64]{1,2,0:T(8,128)}, u32[]{:S(2)}) copy-start(f32[1,2048,64]{1,2,0:T(8,128)} %param.7) | copy-start | bytes 1572868
  0.6 15.7 %copy-start.1 = (bf16[1,64,2048]{2,1,0:T(8,128)(2,1)S(1)}, bf16[1,64,2048]{2,1,0:T(8,128)(2,1)}, u32[]{:S(2)}) copy-start(bf16[1,64,2048]{2,1,0:T(8,128)(2,1)} %param.6) | copy-start | bytes 786436
  138.2 13.4 %copy-start.5 = (f32[1,64,2048]{2,1,0:T(8,128)S(1)}, f32[1,64,2048]{2,1,0:T(8,128)}, u32[]{:S(2)}) copy-start(f32[1,64,2048]{2,1,0:T(8,128)} %param.9) | copy-start | bytes 1572868
  138.2 15.4 %copy-start.6 = (f32[1,64,64]{2,1,0:T(8,128)S(1)}, f32[1,64,64]{2,1,0:T(8,128)}, u32[]{:S(2)}) copy-start(f32[1,64,64]{2,1,0:T(8,128)} %param.10) | copy-start | bytes 49156
  138.2 202.2 %all-to-all-start = ((bf16[32,2,65536]{2,1,0:T(2,128)(2,1)}), bf16[32,2,65536]{2,1,0:T(2,128)(2,1)}, u32[]{:S(2)}, u32[]{:S(2)}) async-start(bf16[32,2,65536]{2,1,0:T(2,128)(2,1)} %reshape.17), calls=%async_computation | async-start | bytes 16777216 | tf_op jit(solution)/shard_map/all_to_all | solution.py:9
  151.7 212.2 %collective-permute-start = (f32[1,64,2048]{2,1,0:T(8,128)S(1)}, f32[1,64,2048]{2,1,0:T(8,128)S(1)}, u32[]{:S(2)}, u32[]{:S(2)}) collective-permute-start(f32[1,64,2048]{2,1,0:T(8,128)S(1)} %copy-done.5), channel_id=1, source_target_pairs={{32,0},{64,32},{96,64},{128,96},{160,128},{192,160},{224,192},{256... | collective-permute-start | bytes 1572872 | tf_op jit(solution)/shard_map/ppermute | solution.py:15
  153.6 7.0 %collective-permute-start.1 = (f32[1,64,64]{2,1,0:T(8,128)S(1)}, f32[1,64,64]{2,1,0:T(8,128)S(1)}, u32[]{:S(2)}, u32[]{:S(2)}) collective-permute-start(f32[1,64,64]{2,1,0:T(8,128)S(1)} %copy-done.6), channel_id=1, source_target_pairs={{32,0},{64,32},{96,64},{128,96},{160,128},{192,160},{224,192},{256... | collective-permute-start | bytes 49160 | tf_op jit(solution)/shard_map/ppermute | solution.py:15
  363.9 33.3 %copy-start.4 = (f32[64,64]{1,0:T(8,128)S(1)}, f32[64,64]{1,0:T(8,128)}, u32[]{:S(2)}) copy-start(f32[64,64]{1,0:T(8,128)} %param.11) | copy-start | bytes 49156
  381.4 77.5 %copy-start.2 = (f32[1,64,2048]{2,1,0:T(8,128)S(1)}, f32[1,64,2048]{2,1,0:T(8,128)}, u32[]{:S(2)}) copy-start(f32[1,64,2048]{2,1,0:T(8,128)} %param.8) | copy-start | bytes 1572868
  383.2 70.8 %all-to-all-start.1 = ((f32[32,1,4096]{2,1,0:T(1,128)}), f32[32,1,4096]{2,1,0:T(1,128)S(1)}, u32[]{:S(2)}, u32[]{:S(2)}) async-start(f32[32,1,4096]{2,1,0:T(1,128)} %reshape.19), calls=%async_computation.1 | async-start | bytes 1048576 | tf_op jit(solution)/shard_map/all_to_all | solution.py:45
  454.0 22.6 %copy-start.3 = (f32[64,64]{1,0:T(8,128)}, f32[64,64]{1,0:T(8,128)S(1)}, u32[]{:S(2)}) copy-start(f32[64,64]{1,0:T(8,128)S(1)} %convolution_add_fusion.1) | copy-start | bytes 49156
